TPU v7x, 128 devices: a whole 4x4x4 slice. The times are simulated.
128 devices in a mesh: row: 16 (over z_lo, y, core), cand: 8 (over z_hi, x).
Axes of the slice: x: 4, y: 4, z: 4 (z_hi: 2, z_lo: 2; z = z_hi * 2 + z_lo), core: 2. Of those that a mesh axis runs over, the one named last changes fastest.
Arguments:
- embeddings: bfloat16 [131072, 768], P('row')
- pick_index: int32 [64], replicated, may hold values from 0 to 131071
- cand_index: int32 [8192], replicated, may hold values from 0 to 131071
Outputs:
- gains: float32 [8192], P('cand')
- coverage: float32 [131072], P('row')
All inputs are finite; a program needn't handle non-finite values.
Results may differ from a plain program's by a relative error of at most 0.0003.
Values may be sent and summed in bfloat16 or wider, within the bound.
A program may use at most 128 MiB of HBM per device.

v0:
```python
import jax
import jax.numpy as jnp
from jax import lax
from jax.sharding import PartitionSpec as P


def select_owned(embeddings, indices):
    count = embeddings.shape[0]
    local = indices - lax.axis_index("row") * count
    owned = (local >= 0) & (local < count)
    taken = jnp.take(embeddings, jnp.clip(local, 0, count - 1), axis=0)
    return jnp.where(owned[:, None], taken, jnp.zeros_like(taken))


def inner(left, right):
    return lax.dot_general(
        left, right, (((1,), (1,)), ((), ())), preferred_element_type=jnp.float32
    )


def per_device(embeddings, pick_index, cand_index):
    count = embeddings.shape[0]
    picked = (
        lax.psum(select_owned(embeddings, pick_index), "row")
        .astype(jnp.float32)
        .astype(jnp.bfloat16)
    )
    coverage = jnp.max(inner(embeddings, picked), axis=1)
    per_column = cand_index.shape[0] // lax.axis_size("cand")
    every = (
        lax.psum(select_owned(embeddings, cand_index), "row")
        .astype(jnp.float32)
        .astype(jnp.bfloat16)
    )
    chosen = lax.dynamic_slice_in_dim(every, lax.axis_index("cand") * per_column, per_column, 0)
    similar = inner(embeddings, chosen)
    partial_gain = jnp.sum(jnp.maximum(similar - coverage[:, None], 0.0), axis=0)
    total_rows = count * lax.axis_size("row")
    gains = lax.psum(partial_gain, "row") / total_rows
    return (gains, coverage)


def solution(mesh):
    return jax.shard_map(
        per_device,
        mesh=mesh,
        in_specs=(P("row", None), P(), P()),
        out_specs=(P("cand"), P("row")),
        check_vma=False,
    )
```

profile of v0, /device:TPU:0, one launch (start us, length us, event | category | flops | bytes accessed | tf_op | source)
XLA Modules:
  0.0 298.8 jit_solution(3463207593277725131)
XLA Ops:
  7.2 0.0 all-reduce.3.cloned.1.call-start
  7.2 0.8 compare_and_fusion.1
  8.0 0.8 fusion.1
  8.8 0.7 compare_and_fusion.2
  9.5 7.0 %gather_fusion.1 = bf16[64,768]{1,0:T(8,128)(2,1)S(1)} fusion(bf16[8192,768]{1,0:T(8,128)(2,1)} %param.3, s32[1024]{0:T(1024)S(1)} %pad_clamp_fusion), kind=kCustom, calls=%fused_computation.1 | custom fusion | bytes 196864 | tf_op jit(solution)/shard_map/jit(_take)/gather | solution.py:11
  16.4 43.3 %gather_fusion = bf16[8192,768]{1,0:T(8,128)(2,1)} fusion(bf16[8192,768]{1,0:T(8,128)(2,1)} %param.3, s32[8192]{0:T(1024)S(1)} %fusion.1), kind=kCustom, calls=%fused_computation | custom fusion | bytes 25198592 | tf_op jit(solution)/shard_map/jit(_take)/gather | solution.py:11
  59.7 0.7 select_select_fusion.1
  60.4 13.0 %select_select_fusion = bf16[8192,768]{1,0:T(8,128)(2,1)} fusion(bf16[8192,768]{1,0:T(8,128)(2,1)} %gather_fusion, pred[8192]{0:T(1024)(128)(4,1)S(1)} %get-tuple-element.7, pred[8192]{0:T(1024)(128)(4,1)S(1)} %get-tuple-element.6), kind=kLoop, calls=%fused_computation.3 | loop fusion | flops 12582912 | bytes 25182208 | tf_op jit(solution)/shard_map/jit(_where)/select_n | solution.py:12
  73.5 0.0 all-reduce.3.cloned.1.call-update
  73.5 163.0 %all-reduce.3.cloned.1.call-done = (bf16[64,768]{1,0:T(8,128)(2,1)}, bf16[8192,768]{1,0:T(8,128)(2,1)}) async-done(((bf16[64,768]{1,0:T(8,128)(2,1)}, bf16[8192,768]{1,0:T(8,128)(2,1)}), (bf16[64,768]{1,0:T(8,128)(2,1)}, bf16[8192,768]{1,0:T(8,128)(2,1)})) %all-reduce.3.cloned.1.call-update) | async-done | bytes 12681232 | tf_op jit(solution)/shard_map/psum | solution.py:24
  236.4 8.5 %convolution_reduce_fusion = f32[8192]{0:T(1024)S(1)} fusion(bf16[64,768]{1,0:T(8,128)(2,1)} %get-tuple-element.2, bf16[8192,768]{1,0:T(8,128)(2,1)} %param.3), kind=kOutput, calls=%fused_computation.5 | convolution fusion | flops 805822464 | bytes 12713984 | tf_op jit(solution)/shard_map/dot_general | solution.py:16
  245.0 0.0 copy-start
  245.0 16.8 %maximum_reduce_fusion = f32[1024]{0:T(1024)S(1)} fusion(bf16[8192,768]{1,0:T(8,128)(2,1)} %param.3, f32[8192]{0:T(1024)S(1)} %convolution_reduce_fusion, bf16[8192,768]{1,0:T(8,128)(2,1)} %get-tuple-element.3, s32[]{:T(128)S(6)} %select_n.32), kind=kOutput, calls=%fused_computation.2 | convolution fusion | flops 12910066688 | bytes 14192644 | tf_op jit(solution)/shard_map/dot_general | solution.py:16
  261.8 0.0 copy-done
  261.8 29.5 %psum.23 = f32[1024]{0:T(1024)S(1)} all-reduce(f32[1024]{0:T(1024)S(1)} %maximum_reduce_fusion), channel_id=1, replica_groups=mesh['row'=16,'cand'=8] {'row'}, use_global_device_ids=true, to_apply=%region_4.5 | all-reduce | flops 1024 | bytes 8192 | tf_op jit(solution)/shard_map/psum | solution.py:39
  291.3 0.6 broadcast_multiply_fusion
  (1 shorter events, 0.0 us)
Async XLA Ops:
  7.2 229.3 %all-reduce.3.cloned.1.call-start = ((), (), s32[]{:S(2)}) async-start(), calls=%async_computation | async-start | bytes 25362432 | tf_op jit(solution)/shard_map/psum | solution.py:24
  245.0 16.8 %copy-start = (f32[8192]{0:T(1024)}, f32[8192]{0:T(1024)S(1)}, u32[]{:S(2)}) copy-start(f32[8192]{0:T(1024)S(1)} %convolution_reduce_fusion) | copy-start | bytes 98308
Sparse Core Ops, SparseCore 0:
  73.6 162.8 all-reduce.2
where the time goes:
time: 299 us
  waiting for transfers between devices  163 us (55%)
  local copies, waits for them, and re-layouts  50.2 us (17%)
  blocking collectives  29.5 us (10%)
  matrix products  25.3 us (8%)
  other arithmetic  16.6 us (6%)
  between operations  14.1 us (5%)
    psum x1, waiting for transfers between devices, per_device(): lax.psum(select_owned(embeddings, pick_index), 'row').astype(jnp.float32)  163 us
    gather x2, local copies, waits for them, and re-layouts, select_owned(): taken = jnp.take(embeddings, jnp.clip(local, 0, count - 1), axis=0)  50.2 us
    psum x1, blocking collectives, per_device(): gains = lax.psum(partial_gain, 'row') / total_rows  29.5 us
    dot_general x2, matrix products, inner(): lax.dot_general(left, right, (((1,), (1,)), ((), ())), preferred_element_...  25.3 us
    select_n x2, other arithmetic, select_owned(): return jnp.where(owned[:, None], taken, jnp.zeros_like(taken))  13.8 us
  transfers between devices with their start and end apart: 1, of which 1 were waited for; matrix products, arithmetic and copies ran while one was open for 0% of the time, Pallas kernels for 0%

commit v1 on v0

--- a/solution.py
+++ b/solution.py
@@ -1,7 +1,17 @@
+import functools
 import jax
 import jax.numpy as jnp
 from jax import lax
 from jax.sharding import PartitionSpec as P
+from jax.lax import all_gather
+
+
+def _guide_record(arr_in, axis_name):
+    carry = all_gather(arr_in, axis_name=axis_name)
+    return jnp.sum(carry, 0)
+
+
+make_strips_all = functools.partial(_guide_record, axis_name="row")
 
 
 def select_owned(embeddings, indices):
@@ -21,7 +31,7 @@
 def per_device(embeddings, pick_index, cand_index):
     count = embeddings.shape[0]
     picked = (
-        lax.psum(select_owned(embeddings, pick_index), "row")
+        make_strips_all(select_owned(embeddings, pick_index))
         .astype(jnp.float32)
         .astype(jnp.bfloat16)
     )

time: 299 us -> 288 us (0.963)
  waiting for transfers between devices: 163 us -> 152 us
    psum x1, waiting for transfers between devices: 163 us -> 151 us  [per_device(): lax.psum(select_owned(embeddings, cand_index), 'row').astype(jnp.float32)]
  transfers between devices with their start and end apart: 1 -> 2, of which waited for: 1 -> 1; matrix products, arithmetic and copies ran while one was open for 0% -> 23% of each run, Pallas kernels for 0% -> 0%
where the time goes in v1:
time: 288 us
  waiting for transfers between devices  152 us (53%)
  local copies, waits for them, and re-layouts  50.2 us (17%)
  blocking collectives  29.4 us (10%)
  matrix products  25.3 us (9%)
  other arithmetic  17.5 us (6%)
  between operations  14.1 us (5%)
    psum x1, waiting for transfers between devices, per_device(): lax.psum(select_owned(embeddings, cand_index), 'row').astype(jnp.float32)  151 us
    gather x2, local copies, waits for them, and re-layouts, select_owned(): taken = jnp.take(embeddings, jnp.clip(local, 0, count - 1), axis=0)  50.2 us
    psum x1, blocking collectives, per_device(): gains = lax.psum(partial_gain, 'row') / total_rows  29.4 us
    dot_general x2, matrix products, inner(): lax.dot_general(left, right, (((1,), (1,)), ((), ())), preferred_element_...  25.3 us
    select_n x2, other arithmetic, select_owned(): return jnp.where(owned[:, None], taken, jnp.zeros_like(taken))  13.8 us
  transfers between devices with their start and end apart: 2, of which 1 were waited for; matrix products, arithmetic and copies ran while one was open for 23% of the time, Pallas kernels for 0%

profile of v1, /device:TPU:0, one launch (start us, length us, event | category | flops | bytes accessed | tf_op | source)
XLA Modules:
  0.0 288.1 jit_solution(3860313337172095971)
XLA Ops:
  7.2 0.0 all-gather.2.cloned.1.call-start
  7.2 0.7 compare_and_fusion.2
  7.9 7.0 %gather_fusion.1 = bf16[64,768]{1,0:T(8,128)(2,1)S(1)} fusion(bf16[8192,768]{1,0:T(8,128)(2,1)} %param.3, s32[1024]{0:T(1024)S(1)} %pad_clamp_fusion), kind=kCustom, calls=%fused_computation.1 | custom fusion | bytes 196864 | tf_op jit(solution)/shard_map/jit(_take)/gather | solution.py:21
  14.9 0.7 fusion.1
  15.6 0.0 all-gather.2.cloned.1.call-update
  15.6 0.0 all-reduce.2.cloned.1.call-start
  15.6 0.8 fusion.2
  16.4 0.0 copy-start
  16.4 43.3 %gather_fusion = bf16[8192,768]{1,0:T(8,128)(2,1)} fusion(bf16[8192,768]{1,0:T(8,128)(2,1)} %param.3, s32[8192]{0:T(1024)S(1)} %fusion.2), kind=kCustom, calls=%fused_computation | custom fusion | bytes 25198592 | tf_op jit(solution)/shard_map/jit(_take)/gather | solution.py:21
  59.7 0.0 copy-done
  59.7 13.1 %select_select_fusion = bf16[8192,768]{1,0:T(8,128)(2,1)} fusion(bf16[8192,768]{1,0:T(8,128)(2,1)} %gather_fusion, pred[8192]{0:T(1024)(128)(4,1)S(1)} %get-tuple-element.5, pred[8192]{0:T(1024)(128)(4,1)S(1)} %get-tuple-element.4), kind=kLoop, calls=%fused_computation.3 | loop fusion | flops 12582912 | bytes 25182208 | tf_op jit(solution)/shard_map/jit(_where)/select_n | solution.py:22
  72.8 0.0 all-reduce.2.cloned.1.call-update
  72.8 0.0 all-gather.2.cloned.1.call-done
  72.8 1.6 reduce_sum.21
  74.5 8.5 %convolution_reduce_fusion = f32[8192]{0:T(1024)S(1)} fusion(bf16[64,768]{1,0:T(8,128)(2,1)S(1)} %reduce_sum.21, bf16[8192,768]{1,0:T(8,128)(2,1)} %param.3), kind=kOutput, calls=%fused_computation.5 | convolution fusion | flops 805822464 | bytes 12713984 | tf_op jit(solution)/shard_map/dot_general | solution.py:26
  82.9 0.0 copy-start.1
  83.0 151.5 %all-reduce.2.cloned.1.call-done = bf16[8192,768]{1,0:T(8,128)(2,1)} async-done(((bf16[8192,768]{1,0:T(8,128)(2,1)}), bf16[8192,768]{1,0:T(8,128)(2,1)}) %all-reduce.2.cloned.1.call-update) | async-done | bytes 12582928 | tf_op jit(solution)/shard_map/psum | solution.py:41
  234.4 16.8 %maximum_reduce_fusion = f32[1024]{0:T(1024)S(1)} fusion(bf16[8192,768]{1,0:T(8,128)(2,1)} %param.3, f32[8192]{0:T(1024)S(1)} %convolution_reduce_fusion, bf16[8192,768]{1,0:T(8,128)(2,1)} %all-reduce.2.cloned.1.call-done, s32[]{:T(128)S(6)} %select_n.46), kind=kOutput, calls=%fused_computation.2 | convolution fusion | flops 12910066688 | bytes 14192644 | tf_op jit(solution)/shard_map/dot_general | solution.py:26
  251.2 0.0 copy-done.1
  251.3 29.4 %psum.15 = f32[1024]{0:T(1024)S(1)} all-reduce(f32[1024]{0:T(1024)S(1)} %maximum_reduce_fusion), channel_id=1, replica_groups=mesh['row'=16,'cand'=8] {'row'}, use_global_device_ids=true, to_apply=%region_4.5 | all-reduce | flops 1024 | bytes 8192 | tf_op jit(solution)/shard_map/psum | solution.py:49
  280.6 0.6 broadcast_multiply_fusion
  (2 shorter events, 0.0 us)
Async XLA Ops:
  7.2 65.7 %all-gather.2.cloned.1.call-start = ((), (), s32[]{:S(2)}) async-start(), calls=%async_computation.1 | async-start | bytes 1671168 | tf_op jit(solution)/shard_map/all_gather | solution.py:10
  15.6 218.8 %all-reduce.2.cloned.1.call-start = ((), (), s32[]{:S(2)}) async-start(), calls=%async_computation | async-start | bytes 25165824 | tf_op jit(solution)/shard_map/psum | solution.py:41
  16.4 43.3 %copy-start = (s32[8192]{0:T(1024)S(1)}, s32[8192]{0:T(1024)}, u32[]{:S(2)}) copy-start(s32[8192]{0:T(1024)} %param.5) | copy-start | bytes 98308
  82.9 168.3 %copy-start.1 = (f32[8192]{0:T(1024)}, f32[8192]{0:T(1024)S(1)}, u32[]{:S(2)}) copy-start(f32[8192]{0:T(1024)S(1)} %convolution_reduce_fusion) | copy-start | bytes 98308
Sparse Core Ops, SparseCore 0:
  15.7 35.6 all-gather.1
  72.9 161.4 all-reduce.1
